TPU v7x, 256 devices: a whole 4x4x8 slice. The times are simulated.
256 devices in a mesh: replica: 8 (over x, z_hi), fsdp: 32 (over y, z_lo, core).
Axes of the slice: x: 4, y: 4, z: 8 (z_hi: 2, z_lo: 4; z = z_hi * 4 + z_lo), core: 2. Of those that a mesh axis runs over, the one named last changes fastest.
Arguments:
- acts: bfloat16 [65536, 2304], P(('replica', 'fsdp')), may hold values from -6 to 6
- value_weight: bfloat16 [2304, 1024], P('fsdp'), may hold values from -0.125 to 0.125
- out_weight: bfloat16 [1024, 2304], P('fsdp'), may hold values from -0.1875 to 0.1875
- norm_gain: float32 [2304], replicated, may hold values from 0.1 to 1.9
- cotan: bfloat16 [65536, 2304], P(('replica', 'fsdp')), may hold values from -6 to 6
Outputs:
- grad_value: float32 [2304, 1024], P('fsdp')
- grad_out: float32 [1024, 2304], P('fsdp')
- grad_acts: bfloat16 [65536, 2304], P(('replica', 'fsdp'))
All inputs are finite; a program needn't handle non-finite values.
Results may differ from a plain program's by a relative error of at most 0.0059.
Values may be sent and summed in bfloat16 or wider, within the bound.
A program may use at most 64 MiB of HBM per device.

v0:
```python
import jax
import jax.numpy as jnp
from jax import lax
from jax.sharding import PartitionSpec as P


def normalize(acts, norm_gain):
    xfloat = acts.astype(jnp.float32)
    inv_rms = lax.rsqrt(jnp.mean(xfloat * xfloat, axis=-1, keepdims=True) + 1e-06)
    normed = (xfloat * inv_rms * norm_gain).astype(jnp.bfloat16)
    return (xfloat, inv_rms, normed)


def times_transposed(left, right):
    return lax.dot_general(
        left, right, (((1,), (1,)), ((), ())), preferred_element_type=jnp.float32
    )


def column_term(left, right):
    return lax.dot_general(
        left, right, (((0,), (0,)), ((), ())), preferred_element_type=jnp.float32
    )


def local(acts, value_weight, out_weight, norm_gain, cotan):
    length = acts.shape[0]
    xfloat, inv_rms, normed = normalize(acts, norm_gain)
    whole_value = lax.all_gather(value_weight, "fsdp", axis=0, tiled=True)
    values = jnp.dot(normed, whole_value, preferred_element_type=jnp.float32).astype(jnp.bfloat16)
    row_index = lax.broadcasted_iota(jnp.int32, (length, length), 0)
    col_index = lax.broadcasted_iota(jnp.int32, (length, length), 1)
    lower_ones = (row_index >= col_index).astype(jnp.bfloat16)
    counts = (lax.broadcasted_iota(jnp.int32, (length, 1), 0) + 1).astype(jnp.float32)
    mixed = (jnp.dot(lower_ones, values, preferred_element_type=jnp.float32) / counts).astype(
        jnp.bfloat16
    )
    whole_out = lax.all_gather(out_weight, "fsdp", axis=0, tiled=True)
    dmix = (times_transposed(cotan, whole_out) / counts).astype(jnp.bfloat16)
    out_share = lax.psum_scatter(column_term(mixed, cotan), "fsdp", scatter_dimension=0, tiled=True)
    out_share = lax.psum(out_share, "replica")
    dvalues = lax.dot_general(
        lower_ones, dmix, (((0,), (0,)), ((), ())), preferred_element_type=jnp.float32
    ).astype(jnp.bfloat16)
    value_share = lax.psum_scatter(
        column_term(normed, dvalues), "fsdp", scatter_dimension=0, tiled=True
    )
    value_share = lax.psum(value_share, "replica")
    dnormed = times_transposed(dvalues, whole_value)
    scaled = norm_gain * dnormed
    dyf = cotan.astype(jnp.float32)
    moment = jnp.mean(scaled * xfloat, axis=-1, keepdims=True)
    grad_acts = dyf + inv_rms * scaled - xfloat * inv_rms * inv_rms * inv_rms * moment
    return (value_share, out_share, grad_acts.astype(jnp.bfloat16))


def solution(mesh):
    placed = (
        P(("replica", "fsdp"), None),
        P("fsdp", None),
        P("fsdp", None),
        P(),
        P(("replica", "fsdp"), None),
    )
    return jax.shard_map(
        local,
        mesh=mesh,
        in_specs=placed,
        out_specs=(P("fsdp", None), P("fsdp", None), P(("replica", "fsdp"), None)),
        check_vma=False,
    )
```

profile of v0, /device:TPU:1, one launch (start us, length us, event | category | flops | bytes accessed | tf_op | source)
XLA Modules:
  0.0 600.5 jit_solution(10199062579357100299)
XLA Ops:
  7.2 0.0 all-gather.3.cloned.1.call-start
  7.2 0.7 all-gather.3.cloned.1.call-update
  7.9 0.0 all-gather.5.cloned.1.call-start
  7.9 0.7 all-gather.5.cloned.1.call-update
  8.6 0.0 reduce-scatter.3.cloned.1.call-start
  8.7 0.0 copy-start
  8.7 0.0 copy-start.2
  8.7 69.3 %all-gather.3.cloned.1.call-done = bf16[1024,2304]{1,0:T(8,128)(2,1)} async-done(((bf16[32,2304]{1,0:T(8,128)(2,1)}), bf16[1024,2304]{1,0:T(8,128)(2,1)}) %all-gather.3.cloned.1.call-update) | async-done | bytes 4718608 | tf_op jit(solution)/shard_map/all_gather | solution.py:38
  78.0 4.3 convolution_convert_fusion.1
  82.4 60.3 %all-gather.5.cloned.1.call-done = bf16[2304,1024]{1,0:T(8,128)(2,1)} async-done(((bf16[72,1024]{1,0:T(8,128)(2,1)}), bf16[2304,1024]{1,0:T(8,128)(2,1)}) %all-gather.5.cloned.1.call-update) | async-done | bytes 4718608 | tf_op jit(solution)/shard_map/all_gather | solution.py:29
  142.7 0.0 copy-done
  142.7 0.0 copy-done.2
  142.7 5.2 fusion.8
  147.9 5.2 fusion.15
  153.1 0.0 reduce-scatter.3.cloned.1.call-update
  153.1 0.0 copy-start.1
  153.1 0.0 reduce-scatter.5.cloned.1.call-start
  153.1 3.9 convolution_convert_fusion
  157.0 0.0 copy-done.1
  157.0 5.4 fusion.11
  162.4 0.0 reduce-scatter.5.cloned.1.call-update
  162.4 0.0 all-reduce.3.cloned.1.call-start
  162.5 150.3 %reduce-scatter.3.cloned.1.call-done = f32[72,1024]{1,0:T(8,128)} async-done(((f32[2304,1024]{1,0:T(8,128)}), f32[72,1024]{1,0:T(8,128)}) %reduce-scatter.3.cloned.1.call-update) | async-done | bytes 294928 | tf_op jit(solution)/shard_map/reduce_scatter | solution.py:45
  312.8 163.2 %reduce-scatter.5.cloned.1.call-done = f32[32,2304]{1,0:T(8,128)} async-done(((f32[1024,2304]{1,0:T(8,128)}), f32[32,2304]{1,0:T(8,128)}) %reduce-scatter.5.cloned.1.call-update) | async-done | bytes 294928 | tf_op jit(solution)/shard_map/reduce_scatter | solution.py:40
  476.0 0.0 all-reduce.3.cloned.1.call-update
  476.0 3.6 fusion.6
  479.6 111.1 %all-reduce.3.cloned.1.call-done = (f32[72,1024]{1,0:T(8,128)}, f32[32,2304]{1,0:T(8,128)}) async-done(((f32[72,1024]{1,0:T(8,128)}, f32[32,2304]{1,0:T(8,128)}), (f32[72,1024]{1,0:T(8,128)}, f32[32,2304]{1,0:T(8,128)})) %all-reduce.3.cloned.1.call-update) | async-done | bytes 589840 | tf_op jit(solution)/shard_map/psum | solution.py:48
  590.6 1.7 copy.10
  592.3 1.7 copy.11
  (3 shorter events, 0.0 us)
Async XLA Ops:
  7.2 70.9 %all-gather.3.cloned.1.call-start = ((), (), s32[]{:S(2)}) async-start(), calls=%async_computation.2 | async-start | bytes 4866048 | tf_op jit(solution)/shard_map/all_gather | solution.py:38
  7.9 134.8 %all-gather.5.cloned.1.call-start = ((), (), s32[]{:S(2)}) async-start(), calls=%async_computation.4 | async-start | bytes 4866048 | tf_op jit(solution)/shard_map/all_gather | solution.py:29
  8.6 304.1 %reduce-scatter.3.cloned.1.call-start = ((), (), s32[]{:S(2)}) async-start(), calls=%async_computation.3 | async-start | bytes 9732096 | tf_op jit(solution)/shard_map/reduce_scatter | solution.py:45
  8.7 134.0 %copy-start = (bf16[256,2304]{1,0:T(8,128)(2,1)S(1)}, bf16[256,2304]{1,0:T(8,128)(2,1)}, u32[]{:S(2)}) copy-start(bf16[256,2304]{1,0:T(8,128)(2,1)} %param.5) | copy-start | bytes 3538948
  8.7 134.0 %copy-start.2 = (f32[2304]{0:T(1024)S(1)}, f32[2304]{0:T(1024)}, u32[]{:S(2)}) copy-start(f32[2304]{0:T(1024)} %param.8) | copy-start | bytes 27652
  153.1 3.9 copy-start.1
  153.1 322.9 %reduce-scatter.5.cloned.1.call-start = ((), (), s32[]{:S(2)}) async-start(), calls=%async_computation.5 | async-start | bytes 9732096 | tf_op jit(solution)/shard_map/reduce_scatter | solution.py:40
  162.4 428.2 %all-reduce.3.cloned.1.call-start = ((), (), s32[]{:S(2)}) async-start(), calls=%async_computation.6 | async-start | bytes 1179648 | tf_op jit(solution)/shard_map/psum | solution.py:48
Sparse Core Ops, SparseCore 0:
  9.9 68.1 all-gather.2
  79.9 62.7 all-gather.4
  153.2 159.5 reduce-scatter.2
  315.2 160.6 reduce-scatter.4
  478.5 112.0 all-reduce.2
where the time goes:
time: 607 us; the launch traced here: 601 us
  waiting for transfers between devices  556 us (92%)
  matrix products  23.9 us (4%)
  between operations  13.8 us (2%)
    reduce_scatter x1, waiting for transfers between devices, local(): lax.psum_scatter(column_term(mixed, cotan), 'fsdp', scatter_dimension=0,...  163 us
    reduce_scatter x1, waiting for transfers between devices, local(): lax.psum_scatter(column_term(normed, dvalues), 'fsdp', scatter_dimension=...  150 us
    psum x1, waiting for transfers between devices, local(): value_share = lax.psum(value_share, 'replica')  111 us
    all_gather x1, waiting for transfers between devices, local(): whole_out = lax.all_gather(out_weight, 'fsdp', axis=0, tiled=True)  69.3 us
    all_gather x1, waiting for transfers between devices, local(): whole_value = lax.all_gather(value_weight, 'fsdp', axis=0, tiled=True)  60.3 us
  transfers between devices with their start and end apart: 5, of which 5 were waited for; matrix products, arithmetic and copies ran while one was open for 3% of the time, Pallas kernels for 0%

commit v1 on v0

v1 whole, which is shorter than its diff:
```python
import functools

import jax
import jax.numpy as jnp
from jax import lax
from jax.experimental import pallas as pl
from jax.experimental.pallas import tpu as pltpu
from jax.sharding import PartitionSpec as P

MESH = pl.DeviceIdType.MESH
BF, F32 = jnp.bfloat16, jnp.float32
D, KVW, TOK = 2304, 1024, 256
HALF_D, HALF_K = D // 2, KVW // 2
N_SEM = 144


def nt(a, b):
    return lax.dot_general(a, b, (((1,), (1,)), ((), ())), preferred_element_type=F32)


def nn(a, b):
    return jnp.dot(a, b, preferred_element_type=F32)


def loop(n, body):
    def step(i, carry):
        body(i)
        return carry

    lax.fori_loop(0, n, step, 0)


def rows(ref, start, size):
    return ref.at[pl.ds(pl.multiple_of(start, 16), size)]


def kernel(
    acts, wv, wo, gain, cotan,
    gv_out, go_out, ga_out,
    cot2, nrm, nrm2, nrmt, inv_ref, wo_a, wo_b, wv_a, wv_b, wvx,
    dmix, dval, vals, mix_t, mix_tb,
    gvq, gx0, gx1, gxl, gxr, gvu, gy0, gy1, gyl, gyr, gvv, gz0, gz1, gzl, gzr, gvw, gvw2, gvf, gvx, gvo,
    go_a, go_b, a0, a1, al, ar, qa, az0, az1, azl, azr,
    b0, b1, bl, br, qb, by0, by1, byl, byr, gos, gosr, got, got2, gof,
    dn_own, dn_send, dn_recv,
    ssem, rsem,
):
    r, f = lax.axis_index("replica"), lax.axis_index("fsdp")
    x, y, zl, c = r // 2, f // 8, (f // 2) % 4, f % 2
    z = (r % 2) * 4 + zl

    def dev(dx=0, dy=0, dz=0, dc=0):
        xx, yy, zz, cc = (x + dx + 4) % 4, (y + dy + 4) % 4, (z + dz + 8) % 8, (c + dc) % 2
        return (xx * 2 + zz // 4, yy * 8 + (zz % 4) * 2 + cc)

    def ydev(s):
        return dev(dy=s)

    def zdev(s):
        return dev(dz=s)

    def xdev(s):
        return dev(dx=s)

    def at4(q, s):
        return (q + s + 4) % 4

    core = dev(dc=1)
    partners = [core, xdev(1), xdev(-1), xdev(2), ydev(1), ydev(-1), zdev(1), zdev(-1), zdev(4)]
    barrier = pltpu.get_barrier_semaphore()
    for p in partners:
        pl.semaphore_signal(barrier, inc=1, device_id=p, device_id_type=MESH)
    pl.semaphore_wait(barrier, len(partners))

    sent = []

    def send(src, dst, to):
        i = len(sent)
        copy = pltpu.make_async_remote_copy(
            src_ref=src, dst_ref=dst, send_sem=ssem.at[i], recv_sem=rsem.at[i],
            device_id=to, device_id_type=MESH,
        )
        copy.start()
        sent.append(copy)
        return copy

    class Gather:
        def __init__(self, buf, size, cut, first, second, slot):
            self.buf, self.size, self.cut = buf, size, cut
            self.first, self.second, self.slot = first, second, slot
            self.p2, self.fw = {}, {}

        def block(self, i, j, half=None):
            start = self.slot(i, j) * self.size
            if half is None:
                return rows(self.buf, start, self.size)
            if half == 0:
                return rows(self.buf, start, self.cut)
            return rows(self.buf, start + self.cut, self.size - self.cut)

        def own(self):
            b = self.block(0, 0)
            self.p1p = send(b, b, self.first(1))
            self.p1m = send(b, b, self.first(-1))
            self.chunk(0)

        def chunk(self, i):
            b = self.block(i, 0)
            self.p2[i] = (send(b, b, self.second(1)), send(b, b, self.second(-1)))

        def near(self):
            self.p1p.wait_recv()
            b = self.block(-1, 0, 0)
            self.f1p = send(b, b, self.first(1))
            self.p1m.wait_recv()
            b = self.block(1, 0, 1)
            self.f1m = send(b, b, self.first(-1))
            self.chunk(-1)
            self.chunk(1)

        def far(self):
            self.f1p.wait_recv()
            self.f1m.wait_recv()
            self.chunk(2)

        def forward(self, i):
            up, down = self.p2[i]
            up.wait_recv()
            b = self.block(i, -1, 0)
            fu = send(b, b, self.second(1))
            down.wait_recv()
            b = self.block(i, 1, 1)
            fd = send(b, b, self.second(-1))
            self.fw[i] = (fu, fd)

        def finish(self):
            for i in (0, -1, 1, 2):
                self.fw[i][0].wait_recv()
                self.fw[i][1].wait_recv()

    def slot_yz(i, j):
        return at4(y, i) * 4 + at4(zl, j)

    def slot_zy(i, j):
        return at4(y, j) * 4 + at4(zl, i)

    class Scatter:
        def __init__(self, part, n, cut, to, q, f0, f1, left, right):
            self.part, self.n, self.cut, self.to, self.q = part, n, cut, to, q
            self.f0, self.f1, self.left, self.right = f0, f1, left, right

        def half(self, s, h):
            start = at4(self.q, s) * self.n
            if h == 0:
                return rows(self.part, start, self.cut)
            return rows(self.part, start + self.cut, self.n - self.cut)

        def open(self):
            n, k = self.n, self.cut
            self.c0 = send(self.half(2, 0), self.f0, self.to(1))
            self.c1 = send(self.half(2, 1), self.f1, self.to(-1))
            self.l1 = send(self.half(1, 1), self.left.at[pl.ds(k, n - k)], self.to(1))
            self.r0 = send(self.half(-1, 0), self.right.at[pl.ds(0, k)], self.to(-1))

        def turn(self):
            n, k = self.n, self.cut
            self.c0.wait_recv()
            h = self.half(1, 0)
            h[...] = (h[...].astype(F32) + self.f0[...].astype(F32)).astype(BF)
            self.l0 = send(h, self.left.at[pl.ds(0, k)], self.to(1))
            self.c1.wait_recv()
            h = self.half(-1, 1)
            h[...] = (h[...].astype(F32) + self.f1[...].astype(F32)).astype(BF)
            self.r1 = send(h, self.right.at[pl.ds(k, n - k)], self.to(-1))

        def close(self, out):
            for copy in (self.l1, self.r0, self.l0, self.r1):
                copy.wait_recv()
            mine = rows(self.part, self.q * self.n, self.n)
            total = mine[...].astype(F32) + self.left[...].astype(F32) + self.right[...].astype(F32)
            out[...] = total.astype(BF).reshape(out.shape)

    me = y * 4 + zl
    rows(wo_a, me * 32, 32)[...] = wo[:, :HALF_D]
    rows(wo_b, me * 32, 32)[...] = wo[:, HALF_D:]
    ga = Gather(wo_a, 32, 16, ydev, zdev, slot_yz)
    gb = Gather(wo_b, 32, 16, zdev, ydev, slot_zy)
    ga.own()
    gb.own()
    cot_copy = send(cotan, cot2, core)

    jj = lax.broadcasted_iota(jnp.int32, (128, 256), 0)
    kk = lax.broadcasted_iota(jnp.int32, (128, 256), 1)
    base = 64 * (jj // 32) + jj % 32

    def picks(which):
        return (kk == base + 32 * which).astype(BF)

    pick_own, pick_other = picks(c), picks(1 - c)
    own_rows = pl.ds(pl.multiple_of(c * 72, 8), 72)
    for q in range(4):
        group = wv[:, 256 * q : 256 * (q + 1)]
        gvx[:, 128 * q : 128 * (q + 1)] = nt(group, pick_other)
        wvx[own_rows, 128 * q : 128 * (q + 1)] = nt(group, pick_own)
    wvx_copy = send(gvx, wvx.at[own_rows], core)

    def norm_step(i):
        at = pl.ds(pl.multiple_of(i * 32, 32), 32)
        xf = acts[at, :].astype(F32)
        inv = lax.rsqrt(jnp.mean(xf * xf, axis=-1, keepdims=True) + 1e-06)
        inv_ref[at, :] = inv
        nrm[at, :] = (xf * inv * gain[...]).astype(BF)

    loop(8, norm_step)
    nrm_copy = send(nrm, nrm2, core)

    ga.near()
    gb.near()
    ga.forward(0)
    gb.forward(0)
    ga.far()
    gb.far()
    for i in (-1, 1):
        ga.forward(i)
        gb.forward(i)

    wvx_copy.wait_recv()
    rows(wv_a, me * 144, 144)[...] = wvx[:, :256].astype(BF)
    rows(wv_b, me * 144, 144)[...] = wvx[:, 256:].astype(BF)
    va = Gather(wv_a, 144, 80, ydev, zdev, slot_yz)
    vb = Gather(wv_b, 144, 80, zdev, ydev, slot_zy)
    ga.forward(2)
    gb.forward(2)
    va.own()
    vb.own()

    def turn_step(src, at):
        def body(t):
            lanes = pl.ds(pl.multiple_of(t * 256, 256), 256)
            nrmt[lanes, at * 256 : (at + 1) * 256] = src[:, lanes].T

        return body

    loop(9, turn_step(nrm, 0))
    nrm_copy.wait_recv()
    loop(9, turn_step(nrm2, 1))
    cot_copy.wait_recv()
    ga.finish()
    gb.finish()

    ri = lax.broadcasted_iota(jnp.int32, (TOK, TOK), 0)
    ci = lax.broadcasted_iota(jnp.int32, (TOK, TOK), 1)
    lower = (ri >= ci).astype(BF)
    upper = (ci >= ri).astype(BF)
    per_count = 1.0 / (lax.broadcasted_iota(jnp.int32, (TOK, 1), 0) + 1).astype(F32)

    for s, cot in enumerate((cotan, cot2)):

        def dmix_step(n, cot=cot, s=s):
            at = pl.ds(pl.multiple_of(n * 256, 256), 256)
            d = nt(cot[:, :HALF_D], wo_a[at, :]) + nt(cot[:, HALF_D:], wo_b[at, :])
            dmix[:, at] = (d * per_count).astype(BF)

        loop(2, dmix_step)
        dval[256 * s : 256 * (s + 1), :] = nn(upper, dmix[...]).astype(BF)
        if s == 0:
            va.near()
            vb.near()

    va.forward(0)
    vb.forward(0)
    va.far()
    vb.far()

    def gv_step(t):
        at = pl.ds(pl.multiple_of(t * 256, 256), 256)
        g = nn(nrmt[at, :], dval[...])
        for q in range(4):
            gvq[pl.ds(pl.multiple_of(q * D + t * 256, 256), 256), :] = g[:, 128 * q : 128 * (q + 1)].astype(BF)

    loop(9, gv_step)
    gvx_rs = Scatter(gvq, D, D // 2, xdev, x, gx0, gx1, gxl, gxr)
    gvx_rs.open()

    for i in (-1, 1, 2):
        va.forward(i)
        vb.forward(i)
    va.finish()
    vb.finish()

    for s, nr in enumerate((nrm, nrm2)):
        vals[:, :256] = nn(nr[...], wv_a[...]).astype(BF)
        vals[:, 256:] = nn(nr[...], wv_b[...]).astype(BF)
        mixed = (nn(lower, vals[...]) * per_count).astype(BF)
        mix_t[:, 256 * s : 256 * (s + 1)] = mixed.T
    for m in range(16):
        yy, zz = m // 4, m % 4
        n = 4 * zz + yy
        mix_tb[32 * n : 32 * (n + 1), :] = mix_t[32 * m : 32 * (m + 1), :]
    for src, dst, lo in ((mix_t, go_a, 0), (mix_tb, go_b, HALF_D)):

        def go_step(n, src=src, dst=dst, lo=lo):
            at = pl.ds(pl.multiple_of(n * 256, 256), 256)
            g = nn(src[at, :256], cotan[:, lo : lo + HALF_D]) + nn(src[at, 256:], cot2[:, lo : lo + HALF_D])
            dst[at, :] = g.astype(BF)

        loop(2, go_step)

    oa = Scatter(go_a, 128, 64, ydev, y, a0, a1, al, ar)
    ob = Scatter(go_b, 128, 64, zdev, zl, b0, b1, bl, br)
    oa.open()
    ob.open()
    gvx_rs.turn()

    def dn_step(t):
        at = pl.ds(pl.multiple_of(t * 256, 256), 256)
        d = nt(dval[:, :256], wv_a[at, :]) + nt(dval[:, 256:], wv_b[at, :])
        dn_own[:, at] = d[:256]
        dn_send[:, at] = d[256:].astype(BF)

    loop(9, dn_step)
    dn_copy = send(dn_send, dn_recv, core)
    oa.turn()
    ob.turn()

    gvx_rs.close(gvu)
    gvy_rs = Scatter(gvu, 576, 288, ydev, y, gy0, gy1, gyl, gyr)
    gvy_rs.open()

    dn_copy.wait_recv()

    def ga_step(i):
        at = pl.ds(pl.multiple_of(i * 32, 32), 32)
        xf, inv = acts[at, :].astype(F32), inv_ref[at, :]
        scaled = gain[...] * (dn_own[at, :] + dn_recv[at, :].astype(F32))
        moment = jnp.mean(scaled * xf, axis=-1, keepdims=True)
        out = cotan[at, :].astype(F32) + inv * scaled - xf * (inv * inv * inv * moment)
        ga_out[at, :] = out.astype(BF)

    loop(8, ga_step)

    oa.close(qa)
    oaz = Scatter(qa, 32, 16, zdev, zl, az0, az1, azl, azr)
    oaz.open()
    ob.close(qb)
    oby = Scatter(qb, 32, 16, ydev, y, by0, by1, byl, byr)
    oby.open()
    gvy_rs.turn()
    oaz.turn()
    oby.turn()
    gvy_rs.close(gvv)
    gvz_rs = Scatter(gvv, 144, 80, zdev, zl, gz0, gz1, gzl, gzr)
    gvz_rs.open()

    oaz.close(gos.at[0:2])
    oby.close(gos.at[2:4])
    cx = [send(gos.at[at4(x, s)], gosr.at[n], xdev(s)) for n, s in enumerate((1, -1, 2))]
    gvz_rs.turn()
    for copy in cx:
        copy.wait_recv()
    t = gos[x].astype(F32) + gosr[0].astype(F32) + gosr[1].astype(F32) + gosr[2].astype(F32)
    got[...] = t.astype(BF)
    ct = send(got, got2, zdev(4))
    gvz_rs.close(gvw)
    cw = send(gvw, gvw2, zdev(4))
    ct.wait_recv()
    gof[x] = (got[...].astype(F32) + got2[...].astype(F32)).astype(BF)
    co = [send(gof.at[x], gof.at[x], xdev(s)) for s in (1, -1, 2)]
    cw.wait_recv()
    gvf[x] = (gvw[...].astype(F32) + gvw2[...].astype(F32)).astype(BF)
    cv = [send(gvf.at[x], gvf.at[x], xdev(s)) for s in (1, -1, 2)]
    for copy in co:
        copy.wait_recv()
    for h in range(2):
        go_out[0:16, HALF_D * h : HALF_D * (h + 1)] = gof[2 * h].astype(F32)
        go_out[16:32, HALF_D * h : HALF_D * (h + 1)] = gof[2 * h + 1].astype(F32)
    for copy in cv:
        copy.wait_recv()
    for q in range(4):
        gvo[0:144, 128 * q : 128 * (q + 1)] = gvf[q].astype(F32)
    cg = send(gvo.at[pl.ds(pl.multiple_of((1 - c) * 72, 8), 72)], gvo.at[pl.ds(144, 72)], core)
    cg.wait_recv()
    for q in range(4):
        lanes = slice(128 * q, 128 * (q + 1))
        own = gvo[own_rows, lanes].astype(BF)
        other = gvo[144:216, lanes].astype(BF)
        gv_out[:, 256 * q : 256 * (q + 1)] = nn(own, pick_own) + nn(other, pick_other)

    for copy in sent:
        copy.wait_send()


def local(acts, value_weight, out_weight, norm_gain, cotan):
    vmem = pl.BlockSpec(memory_space=pltpu.VMEM)

    def bf(*shape):
        return pltpu.VMEM(shape, BF)

    def fl(*shape):
        return pltpu.VMEM(shape, F32)

    scratch = [
        bf(TOK, D), bf(TOK, D), bf(TOK, D), bf(D, 2 * TOK), fl(TOK, 1),
        bf(HALF_K, HALF_D), bf(HALF_K, HALF_D), bf(D, 256), bf(D, 256), fl(144, HALF_K),
        bf(TOK, HALF_K), bf(2 * TOK, HALF_K), bf(TOK, HALF_K), bf(HALF_K, 2 * TOK), bf(HALF_K, 2 * TOK),
        bf(4 * D, 128), bf(1152, 128), bf(1152, 128), bf(D, 128), bf(D, 128),
        bf(D, 128), bf(288, 128), bf(288, 128), bf(576, 128), bf(576, 128),
        bf(576, 128), bf(80, 128), bf(64, 128), bf(144, 128), bf(144, 128),
        bf(144, 128), bf(144, 128), bf(4, 144, 128), fl(72, HALF_K), fl(216, HALF_K),
        bf(HALF_K, HALF_D), bf(HALF_K, HALF_D),
        bf(64, HALF_D), bf(64, HALF_D), bf(128, HALF_D), bf(128, HALF_D),
        bf(128, HALF_D), bf(16, HALF_D), bf(16, HALF_D), bf(32, HALF_D), bf(32, HALF_D),
        bf(64, HALF_D), bf(64, HALF_D), bf(128, HALF_D), bf(128, HALF_D),
        bf(128, HALF_D), bf(16, HALF_D), bf(16, HALF_D), bf(32, HALF_D), bf(32, HALF_D),
        bf(4, 16, HALF_D), bf(3, 16, HALF_D), bf(16, HALF_D), bf(16, HALF_D), bf(4, 16, HALF_D),
        fl(TOK, D), bf(TOK, D), bf(TOK, D),
        pltpu.SemaphoreType.DMA((N_SEM,)), pltpu.SemaphoreType.DMA((N_SEM,)),
    ]
    return pl.pallas_call(
        kernel,
        out_shape=(
            jax.ShapeDtypeStruct((72, KVW), F32),
            jax.ShapeDtypeStruct((32, D), F32),
            jax.ShapeDtypeStruct((TOK, D), BF),
        ),
        in_specs=[vmem] * 5,
        out_specs=(vmem, vmem, vmem),
        scratch_shapes=scratch,
        name="fused",
        compiler_params=pltpu.CompilerParams(
            collective_id=0, has_side_effects=True, vmem_limit_bytes=56 * 2**20
        ),
    )(acts, value_weight, out_weight, norm_gain.reshape(1, D), cotan)


def solution(mesh):
    placed = (
        P(("replica", "fsdp"), None),
        P("fsdp", None),
        P("fsdp", None),
        P(),
        P(("replica", "fsdp"), None),
    )
    return jax.shard_map(
        local,
        mesh=mesh,
        in_specs=placed,
        out_specs=(P("fsdp", None), P("fsdp", None), P(("replica", "fsdp"), None)),
        check_vma=False,
    )
```

time: 607 us -> 95 us (0.16); the launches traced: 601 us -> 94.8 us
  waiting for transfers between devices: 556 us -> 0 us
  Pallas kernels: 0 us -> 88.3 us
  matrix products: 23.9 us -> 0 us
  between operations: 13.8 us -> 0.65 us
    reduce_scatter x2 -> x0, waiting for transfers between devices: 313 us -> none  [the longest x1 163 us: local(): lax.psum_scatter(column_term(mixed, cotan), 'fsdp', scatter_dimension=0,...]
    all_gather x2 -> x0, waiting for transfers between devices: 130 us -> none  [the longest x1 69.3 us: local(): whole_out = lax.all_gather(out_weight, 'fsdp', axis=0, tiled=True)]
    psum x1 -> x0, waiting for transfers between devices: 111 us -> none  [local(): value_share = lax.psum(value_share, 'replica')]
    pallas_call x0 -> x1, Pallas kernels: none -> 88.3 us  [local(): pl.pallas_call(kernel, out_shape=(jax.ShapeDtypeStruct((72, KVW), F32), j...]
    dot_general x5 -> x0, matrix products: 23.9 us -> none  [the longest x2 10.5 us: column_term(): lax.dot_general(left, right, (((0,), (0,)), ((), ())), preferred_element_...]
  transfers between devices with their start and end apart: 5 -> 0, of which waited for: 5 -> 0; matrix products, arithmetic and copies ran while one was open for 3% -> 0% of each run, Pallas kernels for 0% -> 0%
where the time goes in v1:
time: 95 us; the launch traced here: 94.8 us
  Pallas kernels  88.3 us (93%)
  local copies, waits for them, and re-layouts  5.81 us (6%)
    pallas_call x1, Pallas kernels, local(): pl.pallas_call(kernel, out_shape=(jax.ShapeDtypeStruct((72, KVW), F32), j...  88.3 us
    unnamed x5, local copies, waits for them, and re-layouts  4.5 us

profile of v1, /device:TPU:1, one launch (start us, length us, event | category | flops | bytes accessed | tf_op | source)
XLA Modules:
  0.0 94.8 jit_solution(3821108290952919345)
XLA Ops:
  0.6 1.3 %reshape.9.gain = f32[1,2304]{1,0:T(1,128)} reshape(f32[2304]{0:T(1024)} %param.8) | data formatting | bytes 18432 | tf_op jit(solution)/shard_map/reshape | solution.py:433
  1.9 88.3 %fused.1 = (f32[72,1024]{1,0:T(8,128)}, f32[32,2304]{1,0:T(8,128)}, bf16[256,2304]{1,0:T(8,128)(2,1)}) custom-call(bf16[256,2304]{1,0:T(8,128)(2,1)} %acts.1, bf16[72,1024]{1,0:T(8,128)(2,1)} %wv.1, bf16[32,2304]{1,0:T(8,128)(2,1)} %wo.1, f32[1,2304]{1,0:T(1,128)} %reshape.9.gain, bf16[256,2304]{1,0:T(8,128)(2,1)} %cotan.1), custom_call_target="tpu_custom_call" | custom-call | tf_op jit(solution)/shard_map/fused/pallas_call | solution.py:419
  90.3 0.0 copy-start
  90.3 1.8 %copy.11 = f32[72,1024]{1,0:T(8,128)} copy(f32[72,1024]{1,0:T(8,128)} %get-tuple-element.6) | data formatting | bytes 589824
  92.1 1.7 %copy.12 = f32[32,2304]{1,0:T(8,128)} copy(f32[32,2304]{1,0:T(8,128)} %get-tuple-element.7) | data formatting | bytes 589824
  93.7 0.0 copy-done
  93.8 1.0 %copy.13 = bf16[256,2304]{1,0:T(8,128)(2,1)} copy(bf16[256,2304]{1,0:T(8,128)(2,1)S(1)} %copy-done) | data formatting | bytes 2359296
Async XLA Ops:
  90.3 3.5 %copy-start = (bf16[256,2304]{1,0:T(8,128)(2,1)S(1)}, bf16[256,2304]{1,0:T(8,128)(2,1)}, u32[]{:S(2)}) copy-start(bf16[256,2304]{1,0:T(8,128)(2,1)} %get-tuple-element.8) | copy-start | bytes 3538948

commit v2 on v0

v2 whole, which is shorter than its diff:
```python
import math

import jax
import jax.numpy as jnp
from jax import lax
from jax.experimental import pallas as pl
from jax.experimental.pallas import tpu as pltpu
from jax.sharding import PartitionSpec as P

MESH = pl.DeviceIdType.MESH
BF, F32 = jnp.bfloat16, jnp.float32
D, KVW, TOK = 2304, 1024, 256
HALF_D, HALF_K = D // 2, KVW // 2
N_OUT, N_IN = 12, 96
TALLY = 9216


def nt(a, b):
    return lax.dot_general(a, b, (((1,), (1,)), ((), ())), preferred_element_type=F32)


def nn(a, b):
    return jnp.dot(a, b, preferred_element_type=F32)


def loop(n, body):
    def step(i, carry):
        body(i)
        return carry

    lax.fori_loop(0, n, step, 0)


def rows(ref, start, size):
    return ref.at[pl.ds(pl.multiple_of(start, 16), size)]


def kernel(*refs):
    ref = dict(zip(("acts_in", "wv_in", "wo_in", "gain", "cot_in", "gv_out", "go_out", "ga_hbm", *SCRATCH), refs))
    acts_in, wv_in, wo_in, gain, cot_in = (ref[n] for n in ("acts_in", "wv_in", "wo_in", "gain", "cot_in"))
    gv_out, go_out, ga_hbm = (ref[n] for n in ("gv_out", "go_out", "ga_hbm"))
    acts, wv, cotan, cot2, nrm, nrm2, nrmt, inv_ref, wo_a, wo_b, wvf, wvx, wvs = (ref[n] for n in INPUTS)
    dmix, dval, vals, mix_t, mix_tb, dn_own, dn_send, dn_recv, ga_out, tally = (ref[n] for n in WORK)
    gvw, gvw2, fin, got, got2, gof, ssem, rsem, lsem = (ref[n] for n in LAST)
    r, f = lax.axis_index("replica"), lax.axis_index("fsdp")
    x, y, zl, c = r // 2, f // 8, (f // 2) % 4, f % 2
    z = (r % 2) * 4 + zl
    me = y * 4 + zl

    def dev(dx=0, dy=0, dz=0, dc=0):
        xx, yy, zz, cc = (x + dx + 4) % 4, (y + dy + 4) % 4, (z + dz + 8) % 8, (c + dc) % 2
        return (xx * 2 + zz // 4, yy * 8 + (zz % 4) * 2 + cc)

    def ydev(s):
        return dev(dy=s)

    def zdev(s):
        return dev(dz=s)

    def xdev(s):
        return dev(dx=s)

    def at4(q, s):
        return (q + s + 4) % 4

    own_wo = [
        pltpu.make_async_copy(wo_in.at[:, pl.ds(HALF_D * h, HALF_D)], rows(buf, me * 32, 32), lsem.at[h])
        for h, buf in enumerate((wo_a, wo_b))
    ]
    own_wv = pltpu.make_async_copy(wv_in, wv, lsem.at[2])
    own_cot = pltpu.make_async_copy(cot_in, cotan, lsem.at[3])
    own_acts = pltpu.make_async_copy(acts_in, acts, lsem.at[4])
    for copy in (*own_wo, own_wv, own_cot, own_acts):
        copy.start()

    core = dev(dc=1)
    partners = [core, *(xdev(s) for s in (1, -1, 2)), *(dev(dx=s, dc=1) for s in (1, -1, 2))]
    partners += [*(ydev(s) for s in (1, -1, 2)), *(zdev(s) for s in (1, -1, 2, -2, 4))]
    barrier = pltpu.get_barrier_semaphore()
    for p in partners:
        pl.semaphore_signal(barrier, inc=1, device_id=p, device_id_type=MESH)
    pl.semaphore_wait(barrier, len(partners))

    def await_bytes(n, sem):
        view = tally.at[pl.ds(0, n // 256)]
        pltpu.make_async_copy(view, view, sem).wait()

    out_bytes, in_count = [0], [0]

    class Group:
        def __init__(self):
            self.i, self.bytes = in_count[0], 0
            in_count[0] += 1

        def wait(self):
            await_bytes(self.bytes, rsem.at[self.i])

    def send(src, dst, to, group=None):
        n = math.prod(src.shape) * jnp.dtype(src.dtype).itemsize
        if out_bytes[-1] + n > TALLY * 256:
            out_bytes.append(0)
        out_bytes[-1] += n
        alone = group is None
        group = Group() if alone else group
        group.bytes += n
        copy = pltpu.make_async_remote_copy(
            src_ref=src, dst_ref=dst, send_sem=ssem.at[len(out_bytes) - 1], recv_sem=rsem.at[group.i],
            device_id=to, device_id_type=MESH,
        )
        copy.start()
        return copy if alone else None

    class Gather:
        def __init__(self, first, second, block):
            self.first, self.second, self.block = first, second, block
            self.p2, self.rest = {}, Group()

        def spread(self, to, block, near, far):
            b = block(None)
            copies = (send(b, b, to(1), near), send(b, b, to(-1), near))
            if to is zdev:
                h0, h1 = block(0), block(1)
                send(h0, h0, to(2), far)
                send(h1, h1, to(-2), far)
            else:
                send(b, b, to(2), far)
            return copies

        def own(self):
            self.p1far = Group()
            self.p1 = self.spread(self.first, lambda h: self.block(0, 0, h), None, self.p1far)

        def chunk(self, i):
            b = self.block(i, 0, None)
            self.p2[i] = (send(b, b, self.second(1)), send(b, b, self.second(-1)))

        def direct(self, i):
            self.spread(self.second, lambda h: self.block(i, 0, h), self.rest, self.rest)

        def near(self, then):
            self.p1[0].wait_recv()
            then(-1)
            self.p1[1].wait_recv()
            then(1)

        def far(self, then):
            self.p1far.wait()
            then(2)

        def forward(self, i):
            up, down = self.p2[i]
            up.wait_recv()
            b = self.block(i, -1, 0)
            send(b, b, self.second(1), self.rest)
            down.wait_recv()
            b = self.block(i, 1, 1)
            send(b, b, self.second(-1), self.rest)

        def finish(self):
            self.rest.wait()

    def slot_yz(i, j):
        return at4(y, i) * 4 + at4(zl, j)

    def slot_zy(i, j):
        return at4(y, j) * 4 + at4(zl, i)

    def wo_block(buf, slot):
        def block(i, j, half):
            start = slot(i, j) * 32
            if half is None:
                return rows(buf, start, 32)
            return rows(buf, start + 16 * half, 16)

        return block

    def wv_block(slot, lo, n):
        def block(i, j, half):
            at = wvf.at[slot(i, j), pl.ds(lo, n)]
            return at if half is None else at.at[:, pl.ds(256 * half, 256)]

        return block

    def wv_shared(i, j, half):
        at = wvf.at[slot_zy(i, j), pl.ds(pl.multiple_of(16 * x, 16), 16)]
        return at if half is None else at.at[:, pl.ds(256 * half, 256)]

    class Ring:
        def __init__(self, to, part, f0, f1, left, right):
            self.to, self.part = to, part
            self.f0, self.f1, self.left, self.right = f0, f1, left, right

        def recv(self, ref, h):
            return ref.at[pl.ds(2 * h, 2)]

        def open(self):
            self.rest = Group()
            self.c0 = send(self.part(2, 0), self.f0, self.to(1))
            self.c1 = send(self.part(2, 1), self.f1, self.to(-1))
            send(self.part(1, 1), self.recv(self.left, 1), self.to(1), self.rest)
            send(self.part(-1, 0), self.recv(self.right, 0), self.to(-1), self.rest)

        def turn(self):
            self.c0.wait_recv()
            h = self.part(1, 0)
            h[...] = (h[...].astype(F32) + self.f0[...].astype(F32)).astype(BF)
            send(h, self.recv(self.left, 0), self.to(1), self.rest)
            self.c1.wait_recv()
            h = self.part(-1, 1)
            h[...] = (h[...].astype(F32) + self.f1[...].astype(F32)).astype(BF)
            send(h, self.recv(self.right, 1), self.to(-1), self.rest)

        def close(self, out):
            self.rest.wait()
            for h in range(2):
                total = self.part(0, h)[...].astype(F32) + self.recv(self.left, h)[...].astype(F32)
                total += self.recv(self.right, h)[...].astype(F32)
                o = self.recv(out, h)
                o[...] = total.astype(BF)

    class Direct:
        def __init__(self, to, part, left, right, far, halves):
            self.part, self.left, self.right, self.far = part, left, right, far
            self.group = Group()
            send(part(1), left, to(1), self.group)
            send(part(-1), right, to(-1), self.group)
            p = part(2)
            if to is zdev:
                for h, hop in enumerate((2, -2)):
                    send(halves(p, h), halves(far, h), to(hop), self.group)
            else:
                send(p, far, to(2), self.group)

        def close(self, out):
            self.group.wait()
            total = self.part(0)[...].astype(F32) + self.left[...].astype(F32)
            total += self.right[...].astype(F32) + self.far[...].astype(F32)
            out[...] = total.astype(BF)

    def two(p, h):
        return p.at[pl.ds(2 * h, 2)]

    class Reduce:
        def __init__(self, name, halves, outs):
            self.bufs = [[ref[f"{name}{p}_{n}"] for n in PART] for p in range(3)]
            self.halves, self.outs = halves, outs
            bx, by, bz = (b[0] for b in self.bufs)
            self.parts = (
                (xdev, lambda s, h: bx.at[at4(x, s), pl.ds(2 * h, 2)]),
                (ydev, lambda s, h: by.at[pl.ds(2 * h, 2), at4(y, s)]),
                (zdev, lambda s, h: bz.at[pl.ds(2 * h, 2), :, at4(zl, s)]),
            )
            self.rings = [None] * 3

        def open(self, p):
            self.rings[p] = Ring(*self.parts[p], *self.bufs[p][1:5])
            self.rings[p].open()

        def turn(self, p):
            self.rings[p].turn()

        def second(self, p):
            done = self.bufs[p][5]
            self.rings[p].close(done)
            to, part = (
                (ydev, lambda s: done.at[at4(y, s)]),
                (zdev, lambda s: done.at[:, at4(zl, s)]),
                (xdev, lambda s: done.at[at4(x, s)]),
            )[p]
            self.rings[p] = Direct(to, part, *self.bufs[p][6:9], two)

        def third(self, p):
            done = self.bufs[p][9]
            self.rings[p].close(done)
            to, q = ((zdev, zl), (xdev, x), (ydev, y))[p]
            self.rings[p] = Direct(to, lambda s: done.at[at4(q, s)], *self.bufs[p][10:13], self.halves)

        def close(self):
            for p in range(3):
                self.rings[p].close(self.outs(p))

    ga = Gather(ydev, zdev, wo_block(wo_a, slot_yz))
    gb = Gather(zdev, ydev, wo_block(wo_b, slot_zy))
    for copy in own_wo:
        copy.wait()
    ga.own()
    gb.own()
    ga.chunk(0)
    gb.chunk(0)

    jj = lax.broadcasted_iota(jnp.int32, (128, 256), 0)
    kk = lax.broadcasted_iota(jnp.int32, (128, 256), 1)
    base = 64 * (jj // 32) + jj % 32

    def picks(which):
        return (kk == base + 32 * which).astype(BF)

    pick_own, pick_other = picks(c), picks(1 - c)
    own_rows = pl.ds(pl.multiple_of(c * 72, 8), 72)
    own_wv.wait()
    for q in range(4):
        group = wv[:, 256 * q : 256 * (q + 1)]
        wvs[:, 128 * q : 128 * (q + 1)] = nt(group, pick_other)
    wvx_copy = send(wvs, wvx.at[own_rows], core)
    for q in range(4):
        group = wv[:, 256 * q : 256 * (q + 1)]
        wvx[own_rows, 128 * q : 128 * (q + 1)] = nt(group, pick_own)
    own_cot.wait()
    cot_copy = send(cotan, cot2, core)

    own_acts.wait()

    def norm_step(i):
        at = pl.ds(pl.multiple_of(i * 32, 32), 32)
        xf = acts[at, :].astype(F32)
        inv = lax.rsqrt(jnp.mean(xf * xf, axis=-1, keepdims=True) + 1e-06)
        inv_ref[at, :] = inv
        nrm[at, :] = (xf * inv * gain[...].reshape(1, D)).astype(BF)

    loop(8, norm_step)
    nrm_copy = send(nrm, nrm2, core)

    wvx_copy.wait_recv()
    mine = pl.ds(pl.multiple_of(16 * x, 16), 16)
    wvf[me, mine] = wvx[mine, :].astype(BF)
    wvf[me, 64:144] = wvx[64:144].astype(BF)
    vs = Gather(zdev, ydev, wv_shared)
    vs.own()
    vs.direct(0)
    ga.near(ga.chunk)
    gb.near(gb.chunk)
    ga.far(ga.chunk)
    gb.far(gb.chunk)
    ga.forward(0)
    gb.forward(0)
    vs.near(vs.direct)
    vs.far(vs.direct)
    for i in (-1, 1, 2):
        ga.forward(i)
        gb.forward(i)
    va = Gather(ydev, zdev, wv_block(slot_yz, 64, 48))
    vb = Gather(zdev, ydev, wv_block(slot_zy, 112, 32))
    va.own()
    vb.own()
    va.chunk(0)
    vb.chunk(0)

    def turn_step(src, at):
        def body(t):
            lanes = pl.ds(pl.multiple_of(t * 256, 256), 256)
            nrmt[lanes, at * 256 : (at + 1) * 256] = src[:, lanes].T

        return body

    loop(9, turn_step(nrm, 0))
    nrm_copy.wait_recv()
    vs.finish()
    share = wvf.at[:, pl.ds(pl.multiple_of(16 * x, 16), 16)]
    vx = (send(share, share, xdev(1)), send(share, share, xdev(-1)))
    loop(9, turn_step(nrm2, 1))
    cot_copy.wait_recv()
    va.near(va.chunk)
    vb.near(vb.chunk)
    va.far(va.chunk)
    vb.far(vb.chunk)
    ga.finish()
    gb.finish()

    ri = lax.broadcasted_iota(jnp.int32, (TOK, TOK), 0)
    ci = lax.broadcasted_iota(jnp.int32, (TOK, TOK), 1)
    lower = (ri >= ci).astype(BF)
    upper = (ci >= ri).astype(BF)
    per_count = 1.0 / (lax.broadcasted_iota(jnp.int32, (TOK, 1), 0) + 1).astype(F32)

    for s, cot in enumerate((cotan, cot2)):

        def dmix_step(n, cot=cot, s=s):
            at = pl.ds(pl.multiple_of(n * 256, 256), 256)
            d = nt(cot[:, :HALF_D], wo_a[at, :]) + nt(cot[:, HALF_D:], wo_b[at, :])
            dmix[:, at] = (d * per_count).astype(BF)

        loop(2, dmix_step)
        dval[256 * s : 256 * (s + 1), :] = nn(upper, dmix[...]).astype(BF)
        if s == 0:
            va.forward(0)
            vb.forward(0)

    gv = Reduce("gv", lambda p, h: p.at[pl.ds(32 * h, 32 - 16 * h)], lambda p: gvw.at[pl.ds(48 * p, 48)])

    def gv_half(p):
        def body(t):
            at = pl.ds(pl.multiple_of(t * 576, 16), 576)
            g = nn(nrmt[at, :], dval[:, 256 * p : 256 * (p + 1)]).astype(BF)
            for h in range(2):
                block = g[:, 128 * h : 128 * (h + 1)].reshape(4, 144, 128)
                for k in range(3):
                    gv.bufs[k][0][2 * p + h, t] = block[:, 48 * k : 48 * (k + 1)]

        return body

    loop(4, gv_half(0))
    va.forward(-1)
    vb.forward(-1)
    va.forward(1)
    vb.forward(1)
    vx[0].wait_recv()
    half = wvf.at[pl.ds(0, 8), pl.ds(pl.multiple_of(16 * at4(x, -1), 16), 16)]
    vxf = Group()
    send(half, half, xdev(1), vxf)
    vx[1].wait_recv()
    half = wvf.at[pl.ds(8, 8), pl.ds(pl.multiple_of(16 * at4(x, 1), 16), 16)]
    send(half, half, xdev(-1), vxf)
    loop(4, gv_half(1))
    gv.open(0)
    va.forward(2)
    vb.forward(2)
    gv.open(1)
    gv.open(2)
    vxf.wait()
    va.finish()
    vb.finish()

    for s, nr in enumerate((nrm, nrm2)):
        vals[...] = nn(nr[...], wvf[...].reshape(D, HALF_K)).astype(BF)
        mixed = (nn(lower, vals[...]) * per_count).astype(BF)
        mix_t[:, 256 * s : 256 * (s + 1)] = mixed.T
    for m in range(16):
        for u in range(2):
            mix_tb[256 * u + 16 * m : 256 * u + 16 * (m + 1), :] = mix_t[32 * m + 16 * u : 32 * m + 16 * (u + 1), :]
    go = Reduce("go", lambda p, h: p.at[:, pl.ds(256 * h, 256 - 128 * h)], lambda p: got.at[:, pl.ds(384 * p, 384)])
    for h in range(2):
        lo = HALF_D * h
        for u in range(2):
            at = slice(256 * u, 256 * (u + 1))
            g = nn(mix_tb[at, :256], cotan[:, lo : lo + HALF_D]) + nn(mix_tb[at, 256:], cot2[:, lo : lo + HALF_D])
            g = g.astype(BF).reshape(4, 4, 16, HALF_D)
            for k in range(3):
                go.bufs[k][0][2 * u + h] = g[:, :, :, 384 * k : 384 * (k + 1)]
    for p in range(3):
        go.open(p)
    for p in range(3):
        gv.turn(p)

    for s in (1, 0):

        def dn_step(g, s=s):
            w = wvf[pl.ds(8 * g, 8)].reshape(D // 2, HALF_K)
            d = nt(dval[256 * s : 256 * (s + 1), :], w)
            at = pl.ds(pl.multiple_of(g * HALF_D, 128), HALF_D)
            if s == 1:
                dn_send[:, at] = d.astype(BF)
            else:
                dn_own[:, at] = d

        loop(2, dn_step)
        if s == 1:
            dn_copy = send(dn_send, dn_recv, core)
            for p in range(3):
                gv.second(p)
            for p in range(3):
                go.turn(p)
    for p in range(3):
        gv.third(p)
    for p in range(3):
        go.second(p)
    gv.close()
    cw = send(gvw, gvw2, zdev(4))

    dn_copy.wait_recv()

    def ga_step(i):
        at = pl.ds(pl.multiple_of(i * 32, 32), 32)
        xf, inv = acts[at, :].astype(F32), inv_ref[at, :]
        scaled = gain[...].reshape(1, D) * (dn_own[at, :] + dn_recv[at, :].astype(F32))
        moment = jnp.mean(scaled * xf, axis=-1, keepdims=True)
        out = cotan[at, :].astype(F32) + inv * scaled - xf * (inv * inv * inv * moment)
        ga_out[at, :] = out.astype(BF)

    loop(8, ga_step)
    ga_copy = pltpu.make_async_copy(ga_out, ga_hbm, lsem.at[5])
    ga_copy.start()
    for p in range(3):
        go.third(p)

    cw.wait_recv()
    total = (gvw[...].astype(F32) + gvw2[...].astype(F32)).astype(BF).astype(F32)
    fin[c, x] = total
    other_rows = pl.ds(pl.multiple_of((1 - c) * 72, 8), 72)
    keep, give = fin.at[c, x, own_rows], fin.at[c, x, other_rows]
    cv = Group()
    for s in (1, -1, 2):
        send(keep, keep, xdev(s), cv)
    for s in (0, 1, -1, 2):
        send(give, give, dev(dx=s, dc=1), cv)
    go.close()
    ct = send(got, got2, zdev(4))
    cv.wait()
    pick = [picks(0), picks(1)]
    for q in range(4):
        gv_out[:, 256 * q : 256 * (q + 1)] = nn(fin[0, q, own_rows].astype(BF), pick[0]) + nn(
            fin[1, q, own_rows].astype(BF), pick[1]
        )
    ct.wait_recv()
    gof[x] = (got[...].astype(F32) + got2[...].astype(F32)).astype(BF)
    co = Group()
    for s in (1, -1, 2):
        send(gof.at[x], gof.at[x], xdev(s), co)
    ga_copy.wait()
    for k, n in enumerate(out_bytes):
        if k < len(out_bytes) - 1:
            await_bytes(n, ssem.at[k])
    co.wait()
    for u in range(2):
        for h in range(2):
            go_out[16 * u : 16 * (u + 1), HALF_D * h : HALF_D * (h + 1)] = gof[2 * u + h].astype(F32)
    await_bytes(out_bytes[-1], ssem.at[len(out_bytes) - 1])
    assert len(out_bytes) <= N_OUT and in_count[0] <= N_IN, (len(out_bytes), in_count)


def bf(*shape):
    return pltpu.VMEM(shape, BF)


def fl(*shape):
    return pltpu.VMEM(shape, F32)


INPUTS = dict(
    acts=bf(TOK, D), wv=bf(72, KVW), cotan=bf(TOK, D), cot2=bf(TOK, D), nrm=bf(TOK, D), nrm2=bf(TOK, D),
    nrmt=bf(D, 2 * TOK), inv=fl(TOK, 1), wo_a=bf(HALF_K, HALF_D), wo_b=bf(HALF_K, HALF_D),
    wvf=bf(16, 144, HALF_K), wvx=fl(144, HALF_K), wvs=fl(72, HALF_K),
)
WORK = dict(
    dmix=bf(TOK, HALF_K), dval=bf(2 * TOK, HALF_K), vals=bf(TOK, HALF_K), mix_t=bf(HALF_K, 2 * TOK),
    mix_tb=bf(HALF_K, 2 * TOK), dn_own=fl(TOK, D), dn_send=bf(TOK, D), dn_recv=bf(TOK, D), ga=bf(TOK, D),
    tally=bf(TALLY, 128),
)
LAST = dict(
    gvw=bf(144, 128), gvw2=bf(144, 128), fin=fl(2, 4, 144, 128),
    got=bf(16, HALF_D), got2=bf(16, HALF_D), gof=bf(4, 16, HALF_D),
    ssem=pltpu.SemaphoreType.DMA((N_OUT,)), rsem=pltpu.SemaphoreType.DMA((N_IN,)),
    lsem=pltpu.SemaphoreType.DMA((6,)),
)
PART = ("terms", "f0", "f1", "l1", "r1", "d1", "l2", "r2", "m2", "d2", "l3", "r3", "m3")
LEAD = ((4, 4, 4), (2, 4), (2, 4), (4, 4), (4, 4), (4, 4), (4,), (4,), (4,), (4,), (), (), ())
SCRATCH = dict(INPUTS, **WORK, **LAST)
for name, block in (("gv", (48, 128)), ("go", (16, 384))):
    for p in range(3):
        SCRATCH.update({f"{name}{p}_{n}": bf(*lead, *block) for n, lead in zip(PART, LEAD)})


def store(*refs):
    copies = [pltpu.make_async_copy(refs[k], refs[3 + k], refs[6].at[k]) for k in range(3)]
    for copy in copies:
        copy.start()
    for copy in copies:
        copy.wait()


def local(acts, value_weight, out_weight, norm_gain, cotan):
    vmem = pl.BlockSpec(memory_space=pltpu.VMEM)
    anywhere = pl.BlockSpec(memory_space=pl.ANY)
    shapes = (
        jax.ShapeDtypeStruct((72, KVW), F32),
        jax.ShapeDtypeStruct((32, D), F32),
        jax.ShapeDtypeStruct((TOK, D), BF),
    )
    outs = pl.pallas_call(
        kernel,
        out_shape=shapes,
        in_specs=[anywhere, anywhere, anywhere, vmem, anywhere],
        out_specs=(vmem, vmem, anywhere),
        scratch_shapes=list(SCRATCH.values()),
        name="fused",
        compiler_params=pltpu.CompilerParams(
            collective_id=0, has_side_effects=True, vmem_limit_bytes=60 * 2**20
        ),
    )(acts, value_weight, out_weight, norm_gain, cotan)
    return pl.pallas_call(
        store,
        out_shape=shapes,
        in_specs=[vmem] * 3,
        out_specs=(anywhere,) * 3,
        scratch_shapes=[pltpu.SemaphoreType.DMA((3,))],
        name="store",
    )(*outs)


def solution(mesh):
    placed = (
        P(("replica", "fsdp"), None),
        P("fsdp", None),
        P("fsdp", None),
        P(),
        P(("replica", "fsdp"), None),
    )
    return jax.shard_map(
        local,
        mesh=mesh,
        in_specs=placed,
        out_specs=(P("fsdp", None), P("fsdp", None), P(("replica", "fsdp"), None)),
        check_vma=False,
    )
```

time: 607 us -> 80.9 us (0.13)
  waiting for transfers between devices: 556 us -> 0 us
  Pallas kernels: 0 us -> 79.7 us
  matrix products: 23.9 us -> 0 us
  between operations: 13.8 us -> 0.64 us
    reduce_scatter x2 -> x0, waiting for transfers between devices: 313 us -> none  [the longest x1 163 us: local(): lax.psum_scatter(column_term(mixed, cotan), 'fsdp', scatter_dimension=0,...]
    all_gather x2 -> x0, waiting for transfers between devices: 130 us -> none  [the longest x1 69.3 us: local(): whole_out = lax.all_gather(out_weight, 'fsdp', axis=0, tiled=True)]
    psum x1 -> x0, waiting for transfers between devices: 111 us -> none  [local(): value_share = lax.psum(value_share, 'replica')]
    pallas_call x0 -> x2, Pallas kernels: none -> 79.7 us  [the longest x1 77.1 us: local(): pl.pallas_call(kernel, out_shape=shapes, in_specs=[anywhere, anywhere, an...]
    dot_general x5 -> x0, matrix products: 23.9 us -> none  [the longest x2 10.5 us: column_term(): lax.dot_general(left, right, (((0,), (0,)), ((), ())), preferred_element_...]
  transfers between devices with their start and end apart: 5 -> 0, of which waited for: 5 -> 0; matrix products, arithmetic and copies ran while one was open for 3% -> 0% of each run, Pallas kernels for 0% -> 0%
where the time goes in v2:
time: 80.9 us; the launch traced here: 80.4 us
  Pallas kernels  79.7 us (99%)
    pallas_call x1, Pallas kernels, local(): pl.pallas_call(kernel, out_shape=shapes, in_specs=[anywhere, anywhere, an...  77.1 us
    pallas_call x1, Pallas kernels, local(): pl.pallas_call(store, out_shape=shapes, in_specs=[vmem] * 3, out_specs=(a...  2.69 us

profile of v2, /device:TPU:1, one launch (start us, length us, event | category | flops | bytes accessed | tf_op | source)
XLA Modules:
  0.0 80.4 jit_solution(157655954721893917)
XLA Ops:
  0.6 77.1 %fused.1 = (f32[72,1024]{1,0:T(8,128)}, f32[32,2304]{1,0:T(8,128)}, bf16[256,2304]{1,0:T(8,128)(2,1)}) custom-call(bf16[256,2304]{1,0:T(8,128)(2,1)} %refs_0_.1, bf16[72,1024]{1,0:T(8,128)(2,1)} %refs_1_.1, bf16[32,2304]{1,0:T(8,128)(2,1)} %refs_2_.1, f32[2304]{0:T(1024)} %refs_3_.1, bf16[256,2304]{1,0:T(8,128)(2,1)} %refs_4_.1), custom_call_target="tpu_custom_call" | custom-call | tf_op jit(solution)/shard_map/fused/pallas_call | solution.py:568
  77.7 2.7 %store.1 = (f32[72,1024]{1,0:T(8,128)}, f32[32,2304]{1,0:T(8,128)}, bf16[256,2304]{1,0:T(8,128)(2,1)}) custom-call(f32[72,1024]{1,0:T(8,128)} %get-tuple-element.6.refs_0_, f32[32,2304]{1,0:T(8,128)} %get-tuple-element.7.refs_1_, bf16[256,2304]{1,0:T(8,128)(2,1)} %get-tuple-element.8.refs_2_), custom_call_target="tpu_custom_call" | custom-call | tf_op jit(solution)/shard_map/store/pallas_call | solution.py:579

commit v3 on v2

--- a/solution.py
+++ b/solution.py
@@ -39,7 +39,7 @@
     ref = dict(zip(("acts_in", "wv_in", "wo_in", "gain", "cot_in", "gv_out", "go_out", "ga_hbm", *SCRATCH), refs))
     acts_in, wv_in, wo_in, gain, cot_in = (ref[n] for n in ("acts_in", "wv_in", "wo_in", "gain", "cot_in"))
     gv_out, go_out, ga_hbm = (ref[n] for n in ("gv_out", "go_out", "ga_hbm"))
-    acts, wv, cotan, cot2, nrm, nrm2, nrmt, inv_ref, wo_a, wo_b, wvf, wvx, wvs = (ref[n] for n in INPUTS)
+    acts, wv, cotan, cot2, nrm, nrm2, nrmt, inv_ref, wof, wvf, wvx, wvs = (ref[n] for n in INPUTS)
     dmix, dval, vals, mix_t, mix_tb, dn_own, dn_send, dn_recv, ga_out, tally = (ref[n] for n in WORK)
     gvw, gvw2, fin, got, got2, gof, ssem, rsem, lsem = (ref[n] for n in LAST)
     r, f = lax.axis_index("replica"), lax.axis_index("fsdp")
@@ -63,9 +63,10 @@
     def at4(q, s):
         return (q + s + 4) % 4
 
+    own_unit = pl.ds(pl.multiple_of(128 * x, 128), 128)
     own_wo = [
-        pltpu.make_async_copy(wo_in.at[:, pl.ds(HALF_D * h, HALF_D)], rows(buf, me * 32, 32), lsem.at[h])
-        for h, buf in enumerate((wo_a, wo_b))
+        pltpu.make_async_copy(wo_in.at[:, cols], wof.at[me, :, cols], lsem.at[h])
+        for h, cols in enumerate((own_unit, pl.ds(512, D - 512)))
     ]
     own_wv = pltpu.make_async_copy(wv_in, wv, lsem.at[2])
     own_cot = pltpu.make_async_copy(cot_in, cotan, lsem.at[3])
@@ -165,14 +166,16 @@
     def slot_zy(i, j):
         return at4(y, j) * 4 + at4(zl, i)
 
-    def wo_block(buf, slot):
+    def wo_block(slot, lo, n):
         def block(i, j, half):
-            start = slot(i, j) * 32
-            if half is None:
-                return rows(buf, start, 32)
-            return rows(buf, start + 16 * half, 16)
+            at = wof.at[slot(i, j), :, pl.ds(lo, n)]
+            return at if half is None else at.at[pl.ds(16 * half, 16)]
 
         return block
+
+    def wo_shared(i, j, half):
+        at = wof.at[slot_yz(i, j), :, own_unit]
+        return at if half is None else at.at[pl.ds(16 * half, 16)]
 
     def wv_block(slot, lo, n):
         def block(i, j, half):
@@ -184,6 +187,32 @@
     def wv_shared(i, j, half):
         at = wvf.at[slot_zy(i, j), pl.ds(pl.multiple_of(16 * x, 16), 16)]
         return at if half is None else at.at[:, pl.ds(256 * half, 256)]
+
+    class Sum:
+        def __init__(self, own, left, right, far):
+            self.own, self.left, self.right, self.far = own, left, right, far
+            self.group = Group()
+
+        def close(self, out):
+            self.group.wait()
+            total = self.own[...].astype(F32) + self.left[...].astype(F32)
+            total += self.right[...].astype(F32) + self.far[...].astype(F32)
+            out[...] = total.astype(BF)
+
+    def direct(to, part, left, right, far, halves):
+        got_sum = Sum(part(0), left, right, far)
+        send(part(1), left, to(1), got_sum.group)
+        send(part(-1), right, to(-1), got_sum.group)
+        p = part(2)
+        if to is zdev:
+            for h, hop in enumerate((2, -2)):
+                send(halves(p, h), halves(far, h), to(hop), got_sum.group)
+        else:
+            send(p, far, to(2), got_sum.group)
+        return got_sum
+
+    def two(p, h):
+        return p.at[pl.ds(2 * h, 2)]
 
     class Ring:
         def __init__(self, to, part, f0, f1, left, right):
@@ -218,71 +247,86 @@
                 o = self.recv(out, h)
                 o[...] = total.astype(BF)
 
-    class Direct:
-        def __init__(self, to, part, left, right, far, halves):
-            self.part, self.left, self.right, self.far = part, left, right, far
-            self.group = Group()
-            send(part(1), left, to(1), self.group)
-            send(part(-1), right, to(-1), self.group)
-            p = part(2)
-            if to is zdev:
-                for h, hop in enumerate((2, -2)):
-                    send(halves(p, h), halves(far, h), to(hop), self.group)
-            else:
-                send(p, far, to(2), self.group)
-
-        def close(self, out):
-            self.group.wait()
-            total = self.part(0)[...].astype(F32) + self.left[...].astype(F32)
-            total += self.right[...].astype(F32) + self.far[...].astype(F32)
-            out[...] = total.astype(BF)
-
-    def two(p, h):
-        return p.at[pl.ds(2 * h, 2)]
-
     class Reduce:
-        def __init__(self, name, halves, outs):
+        def __init__(self, name, halves):
             self.bufs = [[ref[f"{name}{p}_{n}"] for n in PART] for p in range(3)]
-            self.halves, self.outs = halves, outs
+            self.halves = halves
             bx, by, bz = (b[0] for b in self.bufs)
-            self.parts = (
+            own = (bx.at[x], by.at[:, y], bz.at[:, :, zl])
+            self.sums = [Sum(own[p], *self.bufs[p][1:4]) if name == "go" else None for p in range(3)]
+
+        def open_rings(self):
+            bx, by, bz = (b[0] for b in self.bufs)
+            parts = (
                 (xdev, lambda s, h: bx.at[at4(x, s), pl.ds(2 * h, 2)]),
                 (ydev, lambda s, h: by.at[pl.ds(2 * h, 2), at4(y, s)]),
                 (zdev, lambda s, h: bz.at[pl.ds(2 * h, 2), :, at4(zl, s)]),
             )
-            self.rings = [None] * 3
-
-        def open(self, p):
-            self.rings[p] = Ring(*self.parts[p], *self.bufs[p][1:5])
-            self.rings[p].open()
-
-        def turn(self, p):
-            self.rings[p].turn()
+            for p in range(3):
+                self.sums[p] = Ring(*parts[p], ref[f"gv{p}_f0"], ref[f"gv{p}_f1"], *self.bufs[p][1:3])
+                self.sums[p].open()
+
+        def open_x(self, s):
+            land = {1: 1, -1: 2, 2: 3}[s]
+            send(self.bufs[0][0].at[at4(x, s)], self.bufs[0][land], xdev(s), self.sums[0].group)
+
+        def open_yz(self, units):
+            by, lefty, righty, fary = self.bufs[1][:4]
+            bz, leftz, rightz, farz = self.bufs[2][:4]
+            for s, land in ((2, fary), (1, lefty), (-1, righty)):
+                send(by.at[units, at4(y, s)], land.at[units], ydev(s), self.sums[1].group)
+            for h, hop in enumerate((2, -2)):
+                at = pl.ds(2 * h, 2)
+                send(bz.at[units, at, at4(zl, 2)], farz.at[units, at], zdev(hop), self.sums[2].group)
+            for s, land in ((1, leftz), (-1, rightz)):
+                send(bz.at[units, :, at4(zl, s)], land.at[units], zdev(s), self.sums[2].group)
 
         def second(self, p):
-            done = self.bufs[p][5]
-            self.rings[p].close(done)
+            done = self.bufs[p][4]
+            self.sums[p].close(done)
             to, part = (
                 (ydev, lambda s: done.at[at4(y, s)]),
                 (zdev, lambda s: done.at[:, at4(zl, s)]),
                 (xdev, lambda s: done.at[at4(x, s)]),
             )[p]
-            self.rings[p] = Direct(to, part, *self.bufs[p][6:9], two)
+            self.sums[p] = direct(to, part, *self.bufs[p][5:8], two)
 
         def third(self, p):
-            done = self.bufs[p][9]
-            self.rings[p].close(done)
+            done = self.bufs[p][8]
+            self.sums[p].close(done)
             to, q = ((zdev, zl), (xdev, x), (ydev, y))[p]
-            self.rings[p] = Direct(to, lambda s: done.at[at4(q, s)], *self.bufs[p][10:13], self.halves)
-
-        def close(self):
-            for p in range(3):
-                self.rings[p].close(self.outs(p))
-
-    ga = Gather(ydev, zdev, wo_block(wo_a, slot_yz))
-    gb = Gather(zdev, ydev, wo_block(wo_b, slot_zy))
+            self.sums[p] = direct(to, lambda s: done.at[at4(q, s)], *self.bufs[p][9:12], self.halves)
+
+    gv = Reduce("gv", lambda p, h: p.at[pl.ds(32 * h, 32 - 16 * h)])
+    go = Reduce("go", lambda p, h: p.at[:, pl.ds(256 * h, 256 - 128 * h)])
+
+    class Share:
+        def __init__(self, pick):
+            self.pick, self.rest = pick, Group()
+            p = pick(0, pl.ds(0, 16))
+            self.up, self.down = send(p, p, xdev(1)), send(p, p, xdev(-1))
+
+        def forward(self):
+            self.up.wait_recv()
+            p = self.pick(-1, pl.ds(0, 8))
+            send(p, p, xdev(1), self.rest)
+            self.down.wait_recv()
+            p = self.pick(1, pl.ds(8, 8))
+            send(p, p, xdev(-1), self.rest)
+
+    def wo_units(s, blocks):
+        return wof.at[blocks, :, pl.ds(pl.multiple_of(128 * at4(x, s), 128), 128)]
+
+    def wv_units(s, blocks):
+        return wvf.at[blocks, pl.ds(pl.multiple_of(16 * at4(x, s), 16), 16)]
+
+    gs = Gather(ydev, zdev, wo_shared)
+    ga = Gather(ydev, zdev, wo_block(slot_yz, 512, 896))
+    gb = Gather(zdev, ydev, wo_block(slot_zy, 1408, 896))
     for copy in own_wo:
         copy.wait()
+    gs.own()
+    gs.direct(0)
     ga.own()
     gb.own()
     ga.chunk(0)
@@ -327,44 +371,52 @@
     vs = Gather(zdev, ydev, wv_shared)
     vs.own()
     vs.direct(0)
+    gs.near(gs.direct)
+    gs.far(gs.direct)
     ga.near(ga.chunk)
     gb.near(gb.chunk)
     ga.far(ga.chunk)
     gb.far(gb.chunk)
+    vs.near(vs.direct)
+    vs.far(vs.direct)
     ga.forward(0)
     gb.forward(0)
-    vs.near(vs.direct)
-    vs.far(vs.direct)
-    for i in (-1, 1, 2):
-        ga.forward(i)
-        gb.forward(i)
+    gs.finish()
+    wo_share = Share(wo_units)
+    ga.forward(-1)
+    gb.forward(-1)
+    ga.forward(1)
+    gb.forward(1)
     va = Gather(ydev, zdev, wv_block(slot_yz, 64, 48))
     vb = Gather(zdev, ydev, wv_block(slot_zy, 112, 32))
+
+    def turn_step(src, at):
+        def body(t):
+            lanes = pl.ds(pl.multiple_of(t * 256, 256), 256)
+            nrmt[lanes, at * 256 : (at + 1) * 256] = src[:, lanes].T
+
+        return body
+
+    loop(9, turn_step(nrm, 0))
+    ga.forward(2)
+    gb.forward(2)
     va.own()
     vb.own()
     va.chunk(0)
     vb.chunk(0)
-
-    def turn_step(src, at):
-        def body(t):
-            lanes = pl.ds(pl.multiple_of(t * 256, 256), 256)
-            nrmt[lanes, at * 256 : (at + 1) * 256] = src[:, lanes].T
-
-        return body
-
-    loop(9, turn_step(nrm, 0))
+    wo_share.forward()
+    vs.finish()
+    wv_share = Share(wv_units)
     nrm_copy.wait_recv()
-    vs.finish()
-    share = wvf.at[:, pl.ds(pl.multiple_of(16 * x, 16), 16)]
-    vx = (send(share, share, xdev(1)), send(share, share, xdev(-1)))
     loop(9, turn_step(nrm2, 1))
-    cot_copy.wait_recv()
     va.near(va.chunk)
     vb.near(vb.chunk)
     va.far(va.chunk)
     vb.far(vb.chunk)
+    cot_copy.wait_recv()
     ga.finish()
     gb.finish()
+    wo_share.rest.wait()
 
     ri = lax.broadcasted_iota(jnp.int32, (TOK, TOK), 0)
     ci = lax.broadcasted_iota(jnp.int32, (TOK, TOK), 1)
@@ -376,16 +428,13 @@
 
         def dmix_step(n, cot=cot, s=s):
             at = pl.ds(pl.multiple_of(n * 256, 256), 256)
-            d = nt(cot[:, :HALF_D], wo_a[at, :]) + nt(cot[:, HALF_D:], wo_b[at, :])
+            d = nt(cot[...], wof[pl.ds(8 * n, 8)].reshape(256, D))
             dmix[:, at] = (d * per_count).astype(BF)
 
         loop(2, dmix_step)
         dval[256 * s : 256 * (s + 1), :] = nn(upper, dmix[...]).astype(BF)
-        if s == 0:
-            va.forward(0)
-            vb.forward(0)
-
-    gv = Reduce("gv", lambda p, h: p.at[pl.ds(32 * h, 32 - 16 * h)], lambda p: gvw.at[pl.ds(48 * p, 48)])
+        va.forward((0, -1)[s])
+        vb.forward((0, -1)[s])
 
     def gv_half(p):
         def body(t):
@@ -399,26 +448,16 @@
         return body
 
     loop(4, gv_half(0))
-    va.forward(-1)
-    vb.forward(-1)
     va.forward(1)
     vb.forward(1)
-    vx[0].wait_recv()
-    half = wvf.at[pl.ds(0, 8), pl.ds(pl.multiple_of(16 * at4(x, -1), 16), 16)]
-    vxf = Group()
-    send(half, half, xdev(1), vxf)
-    vx[1].wait_recv()
-    half = wvf.at[pl.ds(8, 8), pl.ds(pl.multiple_of(16 * at4(x, 1), 16), 16)]
-    send(half, half, xdev(-1), vxf)
-    loop(4, gv_half(1))
-    gv.open(0)
+    wv_share.forward()
     va.forward(2)
     vb.forward(2)
-    gv.open(1)
-    gv.open(2)
-    vxf.wait()
+    loop(4, gv_half(1))
+    gv.open_rings()
     va.finish()
     vb.finish()
+    wv_share.rest.wait()
 
     for s, nr in enumerate((nrm, nrm2)):
         vals[...] = nn(nr[...], wvf[...].reshape(D, HALF_K)).astype(BF)
@@ -427,19 +466,20 @@
     for m in range(16):
         for u in range(2):
             mix_tb[256 * u + 16 * m : 256 * u + 16 * (m + 1), :] = mix_t[32 * m + 16 * u : 32 * m + 16 * (u + 1), :]
-    go = Reduce("go", lambda p, h: p.at[:, pl.ds(256 * h, 256 - 128 * h)], lambda p: got.at[:, pl.ds(384 * p, 384)])
-    for h in range(2):
-        lo = HALF_D * h
-        for u in range(2):
-            at = slice(256 * u, 256 * (u + 1))
-            g = nn(mix_tb[at, :256], cotan[:, lo : lo + HALF_D]) + nn(mix_tb[at, 256:], cot2[:, lo : lo + HALF_D])
-            g = g.astype(BF).reshape(4, 4, 16, HALF_D)
-            for k in range(3):
-                go.bufs[k][0][2 * u + h] = g[:, :, :, 384 * k : 384 * (k + 1)]
-    for p in range(3):
-        go.open(p)
-    for p in range(3):
-        gv.turn(p)
+    for s in (2, 1, -1, 0):
+        d = at4(x, s)
+        at = pl.ds(pl.multiple_of(256 * (d // 2), 256), 256)
+        lanes = pl.ds(pl.multiple_of(HALF_D * (d % 2), 128), HALF_D)
+        g = nn(mix_tb[at, :256], cotan[:, lanes]) + nn(mix_tb[at, 256:], cot2[:, lanes])
+        g = g.astype(BF).reshape(4, 4, 16, HALF_D)
+        for k in range(3):
+            go.bufs[k][0][d] = g[:, :, :, 384 * k : 384 * (k + 1)]
+        if s != 0:
+            go.open_x(s)
+        go.open_yz(pl.ds(d, 1))
+
+    for p in range(3):
+        gv.sums[p].turn()
 
     for s in (1, 0):
 
@@ -455,16 +495,8 @@
         loop(2, dn_step)
         if s == 1:
             dn_copy = send(dn_send, dn_recv, core)
-            for p in range(3):
-                gv.second(p)
-            for p in range(3):
-                go.turn(p)
-    for p in range(3):
-        gv.third(p)
-    for p in range(3):
-        go.second(p)
-    gv.close()
-    cw = send(gvw, gvw2, zdev(4))
+    for p in range(3):
+        gv.second(p)
 
     dn_copy.wait_recv()
 
@@ -480,31 +512,41 @@
     ga_copy = pltpu.make_async_copy(ga_out, ga_hbm, lsem.at[5])
     ga_copy.start()
     for p in range(3):
+        go.second(p)
+    for p in range(3):
+        gv.third(p)
+
+    for p in range(3):
         go.third(p)
-
-    cw.wait_recv()
-    total = (gvw[...].astype(F32) + gvw2[...].astype(F32)).astype(BF).astype(F32)
-    fin[c, x] = total
-    other_rows = pl.ds(pl.multiple_of((1 - c) * 72, 8), 72)
-    keep, give = fin.at[c, x, own_rows], fin.at[c, x, other_rows]
+    cw, ct = Group(), Group()
+    for p in range(3):
+        part, land = gvw.at[pl.ds(48 * p, 48)], gvw2.at[pl.ds(48 * p, 48)]
+        gv.sums[p].close(part)
+        send(part, land, zdev(4), cw)
+    for p in range(3):
+        part, land = got.at[:, pl.ds(384 * p, 384)], got2.at[:, pl.ds(384 * p, 384)]
+        go.sums[p].close(part)
+        send(part, land, zdev(4), ct)
+    cw.wait()
+    total = gvw[...].astype(F32) + gvw2[...].astype(F32)
+    for h in range(2):
+        fin[h, c, x, 0:72] = total[72 * h : 72 * (h + 1)].astype(BF)
+    keep, give = fin.at[c, c, x], fin.at[1 - c, c, x]
     cv = Group()
     for s in (1, -1, 2):
         send(keep, keep, xdev(s), cv)
     for s in (0, 1, -1, 2):
         send(give, give, dev(dx=s, dc=1), cv)
-    go.close()
-    ct = send(got, got2, zdev(4))
-    cv.wait()
-    pick = [picks(0), picks(1)]
-    for q in range(4):
-        gv_out[:, 256 * q : 256 * (q + 1)] = nn(fin[0, q, own_rows].astype(BF), pick[0]) + nn(
-            fin[1, q, own_rows].astype(BF), pick[1]
-        )
-    ct.wait_recv()
+    ct.wait()
     gof[x] = (got[...].astype(F32) + got2[...].astype(F32)).astype(BF)
     co = Group()
     for s in (1, -1, 2):
         send(gof.at[x], gof.at[x], xdev(s), co)
+    cv.wait()
+    pick = [picks(0), picks(1)]
+    for q in range(4):
+        g = nn(fin[c, 0, q], pick[0]) + nn(fin[c, 1, q], pick[1])
+        gv_out[:, 256 * q : 256 * (q + 1)] = g[0:72]
     ga_copy.wait()
     for k, n in enumerate(out_bytes):
         if k < len(out_bytes) - 1:
@@ -527,7 +569,7 @@
 
 INPUTS = dict(
     acts=bf(TOK, D), wv=bf(72, KVW), cotan=bf(TOK, D), cot2=bf(TOK, D), nrm=bf(TOK, D), nrm2=bf(TOK, D),
-    nrmt=bf(D, 2 * TOK), inv=fl(TOK, 1), wo_a=bf(HALF_K, HALF_D), wo_b=bf(HALF_K, HALF_D),
+    nrmt=bf(D, 2 * TOK), inv=fl(TOK, 1), wof=bf(16, 32, D),
     wvf=bf(16, 144, HALF_K), wvx=fl(144, HALF_K), wvs=fl(72, HALF_K),
 )
 WORK = dict(
@@ -536,17 +578,19 @@
     tally=bf(TALLY, 128),
 )
 LAST = dict(
-    gvw=bf(144, 128), gvw2=bf(144, 128), fin=fl(2, 4, 144, 128),
+    gvw=bf(144, 128), gvw2=bf(144, 128), fin=bf(2, 2, 4, 80, 128),
     got=bf(16, HALF_D), got2=bf(16, HALF_D), gof=bf(4, 16, HALF_D),
     ssem=pltpu.SemaphoreType.DMA((N_OUT,)), rsem=pltpu.SemaphoreType.DMA((N_IN,)),
     lsem=pltpu.SemaphoreType.DMA((6,)),
 )
-PART = ("terms", "f0", "f1", "l1", "r1", "d1", "l2", "r2", "m2", "d2", "l3", "r3", "m3")
-LEAD = ((4, 4, 4), (2, 4), (2, 4), (4, 4), (4, 4), (4, 4), (4,), (4,), (4,), (4,), (), (), ())
+PART = ("terms", "l1", "r1", "m1", "d1", "l2", "r2", "m2", "d2", "l3", "r3", "m3")
+LEAD = ((4, 4, 4), (4, 4), (4, 4), (4, 4), (4, 4), (4,), (4,), (4,), (4,), (), (), ())
 SCRATCH = dict(INPUTS, **WORK, **LAST)
 for name, block in (("gv", (48, 128)), ("go", (16, 384))):
     for p in range(3):
         SCRATCH.update({f"{name}{p}_{n}": bf(*lead, *block) for n, lead in zip(PART, LEAD)})
+        if name == "gv":
+            SCRATCH.update({f"gv{p}_f{h}": bf(2, 4, *block) for h in range(2)})
 
 
 def store(*refs):

time: 80.9 us -> 75.2 us (0.930)
  Pallas kernels: 79.7 us -> 74.4 us
    pallas_call x1, Pallas kernels: 77.1 us -> 71.7 us  [local(): pl.pallas_call(kernel, out_shape=shapes, in_specs=[anywhere, anywhere, an...]
where the time goes in v3:
time: 75.2 us; the launch traced here: 75.1 us
  Pallas kernels  74.4 us (99%)
    pallas_call x1, Pallas kernels, local(): pl.pallas_call(kernel, out_shape=shapes, in_specs=[anywhere, anywhere, an...  71.7 us
    pallas_call x1, Pallas kernels, local(): pl.pallas_call(store, out_shape=shapes, in_specs=[vmem] * 3, out_specs=(a...  2.69 us

profile of v3, /device:TPU:1, one launch (start us, length us, event | category | flops | bytes accessed | tf_op | source)
XLA Modules:
  0.0 75.1 jit_solution(11277411852354697103)
XLA Ops:
  0.6 71.7 %fused.1 = (f32[72,1024]{1,0:T(8,128)}, f32[32,2304]{1,0:T(8,128)}, bf16[256,2304]{1,0:T(8,128)(2,1)}) custom-call(bf16[256,2304]{1,0:T(8,128)(2,1)} %refs_0_.1, bf16[72,1024]{1,0:T(8,128)(2,1)} %refs_1_.1, bf16[32,2304]{1,0:T(8,128)(2,1)} %refs_2_.1, f32[2304]{0:T(1024)} %refs_3_.1, bf16[256,2304]{1,0:T(8,128)(2,1)} %refs_4_.1), custom_call_target="tpu_custom_call" | custom-call | tf_op jit(solution)/shard_map/fused/pallas_call | solution.py:612
  72.4 2.7 %store.1 = (f32[72,1024]{1,0:T(8,128)}, f32[32,2304]{1,0:T(8,128)}, bf16[256,2304]{1,0:T(8,128)(2,1)}) custom-call(f32[72,1024]{1,0:T(8,128)} %get-tuple-element.6.refs_0_, f32[32,2304]{1,0:T(8,128)} %get-tuple-element.7.refs_1_, bf16[256,2304]{1,0:T(8,128)(2,1)} %get-tuple-element.8.refs_2_), custom_call_target="tpu_custom_call" | custom-call | tf_op jit(solution)/shard_map/store/pallas_call | solution.py:623

commit v4 on v3

--- a/solution.py
+++ b/solution.py
@@ -36,11 +36,11 @@
 
 
 def kernel(*refs):
-    ref = dict(zip(("acts_in", "wv_in", "wo_in", "gain", "cot_in", "gv_out", "go_out", "ga_hbm", *SCRATCH), refs))
-    acts_in, wv_in, wo_in, gain, cot_in = (ref[n] for n in ("acts_in", "wv_in", "wo_in", "gain", "cot_in"))
-    gv_out, go_out, ga_hbm = (ref[n] for n in ("gv_out", "go_out", "ga_hbm"))
-    acts, wv, cotan, cot2, nrm, nrm2, nrmt, inv_ref, wof, wvf, wvx, wvs = (ref[n] for n in INPUTS)
-    dmix, dval, vals, mix_t, mix_tb, dn_own, dn_send, dn_recv, ga_out, tally = (ref[n] for n in WORK)
+    ref = dict(zip(("acts_in", "wv_in", "wo_in", "gain_in", "cot_in", "gv_out", "go_out", "ga_out", *SCRATCH), refs))
+    acts_in, wv_in, wo_in, gain_in, cot_in = (ref[n] for n in ("acts_in", "wv_in", "wo_in", "gain_in", "cot_in"))
+    gv_out, go_out, ga_out = (ref[n] for n in ("gv_out", "go_out", "ga_out"))
+    acts, wv, cotan, gain, cot2, nrm, nrm2, nrmt, inv_ref, wof, wvf, wvx, wvs = (ref[n] for n in INPUTS)
+    dmix, dval, vals, mix_t, mix_tb, dn_own, dn_send, dn_recv, tally = (ref[n] for n in WORK)
     gvw, gvw2, fin, got, got2, gof, ssem, rsem, lsem = (ref[n] for n in LAST)
     r, f = lax.axis_index("replica"), lax.axis_index("fsdp")
     x, y, zl, c = r // 2, f // 8, (f // 2) % 4, f % 2
@@ -71,7 +71,8 @@
     own_wv = pltpu.make_async_copy(wv_in, wv, lsem.at[2])
     own_cot = pltpu.make_async_copy(cot_in, cotan, lsem.at[3])
     own_acts = pltpu.make_async_copy(acts_in, acts, lsem.at[4])
-    for copy in (*own_wo, own_wv, own_cot, own_acts):
+    own_gain = pltpu.make_async_copy(gain_in, gain, lsem.at[5])
+    for copy in (*own_wo, own_wv, own_cot, own_acts, own_gain):
         copy.start()
 
     core = dev(dc=1)
@@ -353,6 +354,7 @@
     cot_copy = send(cotan, cot2, core)
 
     own_acts.wait()
+    own_gain.wait()
 
     def norm_step(i):
         at = pl.ds(pl.multiple_of(i * 32, 32), 32)
@@ -495,9 +497,6 @@
         loop(2, dn_step)
         if s == 1:
             dn_copy = send(dn_send, dn_recv, core)
-    for p in range(3):
-        gv.second(p)
-
     dn_copy.wait_recv()
 
     def ga_step(i):
@@ -509,8 +508,8 @@
         ga_out[at, :] = out.astype(BF)
 
     loop(8, ga_step)
-    ga_copy = pltpu.make_async_copy(ga_out, ga_hbm, lsem.at[5])
-    ga_copy.start()
+    for p in range(3):
+        gv.second(p)
     for p in range(3):
         go.second(p)
     for p in range(3):
@@ -547,7 +546,6 @@
     for q in range(4):
         g = nn(fin[c, 0, q], pick[0]) + nn(fin[c, 1, q], pick[1])
         gv_out[:, 256 * q : 256 * (q + 1)] = g[0:72]
-    ga_copy.wait()
     for k, n in enumerate(out_bytes):
         if k < len(out_bytes) - 1:
             await_bytes(n, ssem.at[k])
@@ -568,13 +566,13 @@
 
 
 INPUTS = dict(
-    acts=bf(TOK, D), wv=bf(72, KVW), cotan=bf(TOK, D), cot2=bf(TOK, D), nrm=bf(TOK, D), nrm2=bf(TOK, D),
+    acts=bf(TOK, D), wv=bf(72, KVW), cotan=bf(TOK, D), gain=fl(D), cot2=bf(TOK, D), nrm=bf(TOK, D), nrm2=bf(TOK, D),
     nrmt=bf(D, 2 * TOK), inv=fl(TOK, 1), wof=bf(16, 32, D),
     wvf=bf(16, 144, HALF_K), wvx=fl(144, HALF_K), wvs=fl(72, HALF_K),
 )
 WORK = dict(
     dmix=bf(TOK, HALF_K), dval=bf(2 * TOK, HALF_K), vals=bf(TOK, HALF_K), mix_t=bf(HALF_K, 2 * TOK),
-    mix_tb=bf(HALF_K, 2 * TOK), dn_own=fl(TOK, D), dn_send=bf(TOK, D), dn_recv=bf(TOK, D), ga=bf(TOK, D),
+    mix_tb=bf(HALF_K, 2 * TOK), dn_own=fl(TOK, D), dn_send=bf(TOK, D), dn_recv=bf(TOK, D),
     tally=bf(TALLY, 128),
 )
 LAST = dict(
@@ -604,20 +602,25 @@
 def local(acts, value_weight, out_weight, norm_gain, cotan):
     vmem = pl.BlockSpec(memory_space=pltpu.VMEM)
     anywhere = pl.BlockSpec(memory_space=pl.ANY)
+    hbm = pl.BlockSpec(memory_space=pltpu.HBM)
     shapes = (
         jax.ShapeDtypeStruct((72, KVW), F32),
         jax.ShapeDtypeStruct((32, D), F32),
         jax.ShapeDtypeStruct((TOK, D), BF),
     )
+    acts, value_weight, out_weight, norm_gain, cotan = (
+        pltpu.with_memory_space_constraint(a, pltpu.HBM)
+        for a in (acts, value_weight, out_weight, norm_gain, cotan)
+    )
     outs = pl.pallas_call(
         kernel,
-        out_shape=shapes,
-        in_specs=[anywhere, anywhere, anywhere, vmem, anywhere],
-        out_specs=(vmem, vmem, anywhere),
+        out_shape=tuple(pltpu.VMEM(shape.shape, shape.dtype) for shape in shapes),
+        in_specs=[hbm] * 5,
+        out_specs=(vmem, vmem, vmem),
         scratch_shapes=list(SCRATCH.values()),
         name="fused",
         compiler_params=pltpu.CompilerParams(
-            collective_id=0, has_side_effects=True, vmem_limit_bytes=60 * 2**20
+            collective_id=0, has_side_effects=True, vmem_limit_bytes=48 * 2**20
         ),
     )(acts, value_weight, out_weight, norm_gain, cotan)
     return pl.pallas_call(
@@ -627,7 +630,7 @@
         out_specs=(anywhere,) * 3,
         scratch_shapes=[pltpu.SemaphoreType.DMA((3,))],
         name="store",
-    )(*outs)
+    )(*(pltpu.with_memory_space_constraint(out, pltpu.VMEM) for out in outs))
 
 
 def solution(mesh):

time: 75.2 us -> 71.7 us (0.953)
  Pallas kernels: 74.4 us -> 71 us
    pallas_call x1, Pallas kernels: 71.7 us -> 69.8 us  [local(): pl.pallas_call(kernel, out_shape=tuple((pltpu.VMEM(shape.shape, shape.dty...]
    pallas_call x1, Pallas kernels: 2.69 us -> 1.24 us  [local(): pl.pallas_call(store, out_shape=shapes, in_specs=[vmem] * 3, out_specs=(a...]
where the time goes in v4:
time: 71.7 us; the launch traced here: 71.6 us
  Pallas kernels  71 us (99%)
    pallas_call x1, Pallas kernels, local(): pl.pallas_call(kernel, out_shape=tuple((pltpu.VMEM(shape.shape, shape.dty...  69.8 us

profile of v4, /device:TPU:1, one launch (start us, length us, event | category | flops | bytes accessed | tf_op | source)
XLA Modules:
  0.0 71.6 jit_solution(17889346640149948869)
XLA Ops:
  0.6 69.8 %fused.1 = (f32[72,1024]{1,0:T(8,128)S(1)}, f32[32,2304]{1,0:T(8,128)S(1)}, bf16[256,2304]{1,0:T(8,128)(2,1)S(1)}) custom-call(bf16[256,2304]{1,0:T(8,128)(2,1)} %refs_0_.1, bf16[72,1024]{1,0:T(8,128)(2,1)} %refs_1_.1, bf16[32,2304]{1,0:T(8,128)(2,1)} %refs_2_.1, f32[2304]{0:T(1024)} %refs_3_.1, bf16[256,2304]{1,0:T(8,128)(2,1)} %refs_4_.1), custom_call_target="tpu_custom_call" | custom-call | tf_op jit(solution)/shard_map/fused/pallas_call | solution.py:615
  70.4 1.2 %store.1 = (f32[72,1024]{1,0:T(8,128)}, f32[32,2304]{1,0:T(8,128)}, bf16[256,2304]{1,0:T(8,128)(2,1)}) custom-call(f32[72,1024]{1,0:T(8,128)S(1)} %get-tuple-element.6.refs_0_, f32[32,2304]{1,0:T(8,128)S(1)} %get-tuple-element.7.refs_1_, bf16[256,2304]{1,0:T(8,128)(2,1)S(1)} %get-tuple-element.8.refs_2_), custom_call_target="tpu_custom_call" | custom-call | tf_op jit(solution)/shard_map/store/pallas_call | solution.py:626

commit v5 on v4

--- a/solution.py
+++ b/solution.py
@@ -11,7 +11,7 @@
 BF, F32 = jnp.bfloat16, jnp.float32
 D, KVW, TOK = 2304, 1024, 256
 HALF_D, HALF_K = D // 2, KVW // 2
-N_OUT, N_IN = 12, 96
+N_OUT, N_IN = 7, 94
 TALLY = 9216
 
 
@@ -63,6 +63,13 @@
     def at4(q, s):
         return (q + s + 4) % 4
 
+    core = dev(dc=1)
+    partners = [core, *(xdev(s) for s in (1, -1, 2)), *(dev(dx=s, dc=1) for s in (1, -1, 2))]
+    partners += [*(ydev(s) for s in (1, -1, 2)), *(zdev(s) for s in (1, -1, 2, -2, 4))]
+    barrier = pltpu.get_barrier_semaphore()
+    for p in partners:
+        pl.semaphore_signal(barrier, inc=1, device_id=p, device_id_type=MESH)
+
     own_unit = pl.ds(pl.multiple_of(128 * x, 128), 128)
     own_wo = [
         pltpu.make_async_copy(wo_in.at[:, cols], wof.at[me, :, cols], lsem.at[h])
@@ -75,12 +82,6 @@
     for copy in (*own_wo, own_wv, own_cot, own_acts, own_gain):
         copy.start()
 
-    core = dev(dc=1)
-    partners = [core, *(xdev(s) for s in (1, -1, 2)), *(dev(dx=s, dc=1) for s in (1, -1, 2))]
-    partners += [*(ydev(s) for s in (1, -1, 2)), *(zdev(s) for s in (1, -1, 2, -2, 4))]
-    barrier = pltpu.get_barrier_semaphore()
-    for p in partners:
-        pl.semaphore_signal(barrier, inc=1, device_id=p, device_id_type=MESH)
     pl.semaphore_wait(barrier, len(partners))
 
     def await_bytes(n, sem):

time: 71.7 us -> 71.5 us (level)
  no operation moved by 1% of the time
where the time goes in v5:
time: 71.5 us; the launch traced here: 71.4 us
  Pallas kernels  70.7 us (99%)
    pallas_call x1, Pallas kernels, local(): pl.pallas_call(kernel, out_shape=tuple((pltpu.VMEM(shape.shape, shape.dty...  69.5 us

profile of v5, /device:TPU:1, one launch (start us, length us, event | category | flops | bytes accessed | tf_op | source)
XLA Modules:
  0.0 71.4 jit_solution(13155927635512234780)
XLA Ops:
  0.6 69.5 %fused.1 = (f32[72,1024]{1,0:T(8,128)S(1)}, f32[32,2304]{1,0:T(8,128)S(1)}, bf16[256,2304]{1,0:T(8,128)(2,1)S(1)}) custom-call(bf16[256,2304]{1,0:T(8,128)(2,1)} %refs_0_.1, bf16[72,1024]{1,0:T(8,128)(2,1)} %refs_1_.1, bf16[32,2304]{1,0:T(8,128)(2,1)} %refs_2_.1, f32[2304]{0:T(1024)} %refs_3_.1, bf16[256,2304]{1,0:T(8,128)(2,1)} %refs_4_.1), custom_call_target="tpu_custom_call" | custom-call | tf_op jit(solution)/shard_map/fused/pallas_call | solution.py:616
  70.1 1.2 %store.1 = (f32[72,1024]{1,0:T(8,128)}, f32[32,2304]{1,0:T(8,128)}, bf16[256,2304]{1,0:T(8,128)(2,1)}) custom-call(f32[72,1024]{1,0:T(8,128)S(1)} %get-tuple-element.6.refs_0_, f32[32,2304]{1,0:T(8,128)S(1)} %get-tuple-element.7.refs_1_, bf16[256,2304]{1,0:T(8,128)(2,1)S(1)} %get-tuple-element.8.refs_2_), custom_call_target="tpu_custom_call" | custom-call | tf_op jit(solution)/shard_map/store/pallas_call | solution.py:627
